TPU v7x, 32 devices: a whole 2x2x4 slice. The times are simulated.
32 devices in a mesh: row: 8 (over z, y), col: 4 (over x, core).
Axes of the slice: x: 2, y: 2, z: 4, core: 2. Of those that a mesh axis runs over, the one named last changes fastest.
Arguments:
- tokens: bfloat16 [1024, 4096], P('row', 'col'), may hold values from -6 to 6
- w_in: bfloat16 [4096, 16384], P('col', 'row'), may hold values from -0.09375 to 0.09375
- w_out: bfloat16 [16384, 4096], P('row', 'col'), may hold values from -0.046875 to 0.046875
- cotangent: bfloat16 [1024, 4096], P('row', 'col'), may hold values from -6 to 6
Outputs:
- block_out: bfloat16 [1024, 4096], P(('row', 'col'))
- grad_tokens: bfloat16 [1024, 4096], P('row', 'col')
- grad_in: float32 [4096, 16384], P('col', 'row')
- grad_out: float32 [16384, 4096], P('row', 'col')
All inputs are finite; a program needn't handle non-finite values.
Results may differ from a plain program's by a relative error of at most 0.015.
Values may be sent and summed in bfloat16 or wider, within the bound.
No kernel may reach another device: no remote copies, remote signals or barrier semaphores. Data moves between devices by JAX's collectives and lax.ppermute only.
A program may use at most 128 MiB of HBM per device.

v0:
```python
import jax
import jax.numpy as jnp
from jax import lax
from jax.sharding import PartitionSpec as P


def gelu_grad(value):
    cdf = 0.5 * (1.0 + jax.scipy.special.erf(value * 0.7071067811865476))
    pdf = jnp.exp(-0.5 * value * value) * 0.3989422804014327
    return cdf + value * pdf


def token_panel(local_rows):
    return lax.all_gather(local_rows, "row", axis=0, tiled=True)


def hidden_panel(local_rows):
    return lax.all_gather(local_rows, "col", axis=0, tiled=True)


def contract_last(left, right):
    return lax.dot_general(
        left, right, (((1,), (1,)), ((), ())), preferred_element_type=jnp.float32
    )


def width_split(left_all, right, transposed):

    def width_term():
        if transposed:
            return contract_last(left_all, right)
        return jnp.dot(left_all, right, preferred_element_type=jnp.float32)

    return lax.psum_scatter(
        width_term().astype(jnp.bfloat16), "col", scatter_dimension=0, tiled=True
    ).astype(jnp.float32)


def unit_sum(left_all, right, transposed):

    def unit_term():
        if transposed:
            return contract_last(left_all, right)
        return jnp.dot(left_all, right, preferred_element_type=jnp.float32)

    return lax.psum_scatter(
        unit_term().astype(jnp.bfloat16), "row", scatter_dimension=0, tiled=True
    ).astype(jnp.float32)


def local(tokens, w_in, w_out, cotangent):
    tokens_all = token_panel(tokens)
    upstream_all = token_panel(cotangent)
    pre_part = width_split(tokens_all, w_in, False)
    act_all = hidden_panel(jax.nn.gelu(pre_part, approximate=False).astype(jnp.bfloat16))
    dact_part = width_split(upstream_all, w_out, True)
    dpre_all = hidden_panel((dact_part * gelu_grad(pre_part)).astype(jnp.bfloat16))
    mixed = unit_sum(act_all, w_out, False)
    block_rows = (tokens.astype(jnp.float32) + mixed).astype(jnp.bfloat16)
    block_out = lax.all_to_all(block_rows, "col", split_axis=0, concat_axis=1, tiled=True)
    grad_out = lax.dot_general(
        act_all, upstream_all, (((0,), (0,)), ((), ())), preferred_element_type=jnp.float32
    )
    grad_in = lax.dot_general(
        tokens_all, dpre_all, (((0,), (0,)), ((), ())), preferred_element_type=jnp.float32
    )
    back = unit_sum(dpre_all, w_in, True)
    grad_tokens = (cotangent.astype(jnp.float32) + back).astype(jnp.bfloat16)
    return (block_out, grad_tokens, grad_in, grad_out)


def solution(mesh):
    in_specs = (P("row", "col"), P("col", "row"), P("row", "col"), P("row", "col"))
    out_specs = (P(("row", "col"), None), P("row", "col"), P("col", "row"), P("row", "col"))
    return jax.shard_map(local, mesh=mesh, in_specs=in_specs, out_specs=out_specs, check_vma=False)
```

profile of v0, /device:TPU:0, one launch (start us, length us, event | category | flops | bytes accessed | tf_op | source)
XLA Modules:
  0.0 435.8 jit_solution(15822295467766029946)
XLA Ops:
  7.2 0.7 all-gather.5.cloned.1.call-update
  7.9 0.7 all-gather.9.cloned.1.call-update
  8.7 53.5 %all-gather.5.cloned.1.call-done = bf16[1024,1024]{1,0:T(8,128)(2,1)} async-done(((bf16[128,1024]{1,0:T(8,128)(2,1)}), bf16[1024,1024]{1,0:T(8,128)(2,1)}) %all-gather.5.cloned.1.call-update) | async-done | bytes 2097168 | tf_op jit(solution)/shard_map/all_gather | solution.py:14
  62.1 9.3 %convolution_convert_fusion.1 = bf16[1024,2048]{1,0:T(8,128)(2,1)} fusion(bf16[1024,1024]{1,0:T(8,128)(2,1)} %all-gather.5.cloned.1.call-done, bf16[1024,2048]{1,0:T(8,128)(2,1)} %param.5), kind=kOutput, calls=%fused_computation.8 | convolution fusion | flops 4297064448 | bytes 10485760 | tf_op jit(solution)/shard_map/dot_general | solution.py:32
  71.6 40.5 %all-gather.9.cloned.1.call-done = bf16[1024,1024]{1,0:T(8,128)(2,1)} async-done(((bf16[128,1024]{1,0:T(8,128)(2,1)}), bf16[1024,1024]{1,0:T(8,128)(2,1)}) %all-gather.9.cloned.1.call-update) | async-done | bytes 2097168 | tf_op jit(solution)/shard_map/all_gather | solution.py:14
  112.1 9.4 %convolution_convert_fusion = bf16[1024,2048]{1,0:T(8,128)(2,1)} fusion(bf16[1024,1024]{1,0:T(8,128)(2,1)} %all-gather.9.cloned.1.call-done, bf16[2048,1024]{1,0:T(8,128)(2,1)} %param.6), kind=kOutput, calls=%fused_computation.7 | convolution fusion | flops 4297064448 | bytes 10485760 | tf_op jit(solution)/shard_map/dot_general | solution.py:22
  121.5 36.7 %reduce-scatter.5.cloned.1.call-done = bf16[256,2048]{1,0:T(8,128)(2,1)} async-done(((bf16[1024,2048]{1,0:T(8,128)(2,1)}), bf16[256,2048]{1,0:T(8,128)(2,1)}) %reduce-scatter.5.cloned.1.call-update) | async-done | bytes 1048592 | tf_op jit(solution)/shard_map/reduce_scatter | solution.py:34
  158.2 47.7 %reduce-scatter.9.cloned.1.call-done = bf16[256,2048]{1,0:T(8,128)(2,1)} async-done(((bf16[1024,2048]{1,0:T(8,128)(2,1)}), bf16[256,2048]{1,0:T(8,128)(2,1)}) %reduce-scatter.9.cloned.1.call-update) | async-done | bytes 1048592 | tf_op jit(solution)/shard_map/reduce_scatter | solution.py:34
  205.9 7.3 %fusion.38 = (bf16[256,2048]{1,0:T(8,128)(2,1)}, bf16[256,2048]{1,0:T(8,128)(2,1)}) fusion(bf16[256,2048]{1,0:T(8,128)(2,1)} %reduce-scatter.5.cloned.1.call-done, bf16[256,2048]{1,0:T(8,128)(2,1)} %reduce-scatter.9.cloned.1.call-done), kind=kLoop, calls=%fused_computation.48 | loop fusion | flops 40370176 | bytes 4194304 | tf_op jit(solution)/shard_map/convert_element_type | solution.py:57
  213.3 0.5 all-gather.11.cloned.1.call-update
  213.8 34.0 %all-gather.7.cloned.1.call-done = bf16[1024,2048]{1,0:T(8,128)(2,1)} async-done(((bf16[256,2048]{1,0:T(8,128)(2,1)}), bf16[1024,2048]{1,0:T(8,128)(2,1)}) %all-gather.7.cloned.1.call-update) | async-done | bytes 4194320 | tf_op jit(solution)/shard_map/all_gather | solution.py:18
  247.9 9.3 %convolution_convert_fusion.3 = bf16[1024,1024]{1,0:T(8,128)(2,1)} fusion(bf16[1024,2048]{1,0:T(8,128)(2,1)} %all-gather.7.cloned.1.call-done, bf16[2048,1024]{1,0:T(8,128)(2,1)} %param.6), kind=kOutput, calls=%fused_computation.50 | convolution fusion | flops 4296015872 | bytes 10485760 | tf_op jit(solution)/shard_map/dot_general | solution.py:44
  257.4 26.9 %all-gather.11.cloned.1.call-done = bf16[1024,2048]{1,0:T(8,128)(2,1)} async-done(((bf16[256,2048]{1,0:T(8,128)(2,1)}), bf16[1024,2048]{1,0:T(8,128)(2,1)}) %all-gather.11.cloned.1.call-update) | async-done | bytes 4194320 | tf_op jit(solution)/shard_map/all_gather | solution.py:18
  284.4 9.3 %convolution_convert_fusion.2 = bf16[1024,1024]{1,0:T(8,128)(2,1)} fusion(bf16[1024,2048]{1,0:T(8,128)(2,1)} %all-gather.11.cloned.1.call-done, bf16[1024,2048]{1,0:T(8,128)(2,1)} %param.5), kind=kOutput, calls=%fused_computation.49 | convolution fusion | flops 4296015872 | bytes 10485760 | tf_op jit(solution)/shard_map/dot_general | solution.py:22
  293.7 1.6 copy-done.2
  295.3 9.0 %convolution_bitcast_fusion = f32[1024,2048]{0,1:T(8,128)} fusion(bf16[1024,2048]{1,0:T(8,128)(2,1)} %all-gather.11.cloned.1.call-done, bf16[1024,1024]{1,0:T(8,128)(2,1)S(1)} %copy-done.2), kind=kOutput, calls=%fused_computation.6 | convolution fusion | flops 4294967296 | bytes 14680064 | tf_op jit(solution)/shard_map/dot_general | solution.py:64
  304.3 9.3 %copy.9 = f32[1024,2048]{1,0:T(8,128)} copy(f32[1024,2048]{0,1:T(8,128)} %convolution_bitcast_fusion) | data formatting | bytes 16777216
  313.7 9.1 %fusion.39 = f32[2048,1024]{1,0:T(8,128)} fusion(bf16[1024,2048]{1,0:T(8,128)(2,1)} %all-gather.7.cloned.1.call-done, bf16[1024,1024]{1,0:T(8,128)(2,1)S(1)} %copy-done.3), kind=kOutput, calls=%fused_computation.53 | convolution fusion | flops 4294967296 | bytes 14680064 | tf_op jit(solution)/shard_map/dot_general | solution.py:61
  322.8 33.2 %reduce-scatter.7.cloned.1.call-done = bf16[128,1024]{1,0:T(8,128)(2,1)} async-done(((bf16[1024,1024]{1,0:T(8,128)(2,1)}), bf16[128,1024]{1,0:T(8,128)(2,1)}) %reduce-scatter.7.cloned.1.call-update) | async-done | bytes 262160 | tf_op jit(solution)/shard_map/reduce_scatter | solution.py:46
  356.0 1.7 add_convert_fusion.1
  357.7 3.4 all-to-all-start
  361.1 65.4 %reduce-scatter.11.cloned.1.call-done = bf16[128,1024]{1,0:T(8,128)(2,1)} async-done(((bf16[1024,1024]{1,0:T(8,128)(2,1)}), bf16[128,1024]{1,0:T(8,128)(2,1)}) %reduce-scatter.11.cloned.1.call-update) | async-done | bytes 262160 | tf_op jit(solution)/shard_map/reduce_scatter | solution.py:46
  426.5 1.7 add_convert_fusion
  428.2 0.7 copy.10
  (21 shorter events, 0.6 us)
Async XLA Ops:
  7.2 55.0 %all-gather.5.cloned.1.call-start = ((), (), s32[]{:S(2)}) async-start(), calls=%async_computation.5 | async-start | bytes 2359296 | tf_op jit(solution)/shard_map/all_gather | solution.py:14
  7.9 104.2 %all-gather.9.cloned.1.call-start = ((), (), s32[]{:S(2)}) async-start(), calls=%async_computation.9 | async-start | bytes 2359296 | tf_op jit(solution)/shard_map/all_gather | solution.py:14
  8.6 149.6 %reduce-scatter.5.cloned.1.call-start = ((), (), s32[]{:S(2)}) async-start(), calls=%async_computation.6 | async-start | bytes 5242880 | tf_op jit(solution)/shard_map/reduce_scatter | solution.py:34
  71.5 134.4 %reduce-scatter.9.cloned.1.call-start = ((), (), s32[]{:S(2)}) async-start(), calls=%async_computation.10 | async-start | bytes 5242880 | tf_op jit(solution)/shard_map/reduce_scatter | solution.py:34
  121.5 126.4 %all-gather.7.cloned.1.call-start = ((), (), s32[]{:S(2)}) async-start(), calls=%async_computation.7 | async-start | bytes 5242880 | tf_op jit(solution)/shard_map/all_gather | solution.py:18
  213.2 71.1 %all-gather.11.cloned.1.call-start = ((), (), s32[]{:S(2)}) async-start(), calls=%async_computation.11 | async-start | bytes 5242880 | tf_op jit(solution)/shard_map/all_gather | solution.py:18
  213.8 142.2 %reduce-scatter.7.cloned.1.call-start = ((), (), s32[]{:S(2)}) async-start(), calls=%async_computation.8 | async-start | bytes 2359296 | tf_op jit(solution)/shard_map/reduce_scatter | solution.py:46
  257.2 169.3 %reduce-scatter.11.cloned.1.call-start = ((), (), s32[]{:S(2)}) async-start(), calls=%async_computation.12 | async-start | bytes 2359296 | tf_op jit(solution)/shard_map/reduce_scatter | solution.py:46
  293.7 1.7 copy-start.2
  304.3 9.3 %copy-start.3 = (bf16[1024,1024]{1,0:T(8,128)(2,1)S(1)}, bf16[1024,1024]{1,0:T(8,128)(2,1)}, u32[]{:S(2)}) copy-start(bf16[1024,1024]{1,0:T(8,128)(2,1)} %all-gather.9.cloned.1.call-done) | copy-start | bytes 6291460
  313.7 42.3 %copy-start = (bf16[128,1024]{1,0:T(8,128)(2,1)S(1)}, bf16[128,1024]{1,0:T(8,128)(2,1)}, u32[]{:S(2)}) copy-start(bf16[128,1024]{1,0:T(8,128)(2,1)} %param.4) | copy-start | bytes 786436
  313.7 112.8 %copy-start.1 = (bf16[128,1024]{1,0:T(8,128)(2,1)S(1)}, bf16[128,1024]{1,0:T(8,128)(2,1)}, u32[]{:S(2)}) copy-start(bf16[128,1024]{1,0:T(8,128)(2,1)} %param.7) | copy-start | bytes 786436
  357.7 70.5 %all-to-all-start = ((bf16[4,32,1024]{2,1,0:T(8,128)(2,1)}), bf16[4,32,1024]{2,1,0:T(8,128)(2,1)S(1)}, u32[]{:S(2)}, u32[]{:S(2)}) async-start(bf16[4,32,1024]{2,1,0:T(8,128)(2,1)} %bitcast), calls=%async_computation.2 | async-start | bytes 524288 | tf_op jit(solution)/shard_map/all_to_all | solution.py:60
Sparse Core Ops, SparseCore 0:
  10.1 51.9 all-gather.4
  64.3 47.7 all-gather.8
  115.2 43.0 reduce-scatter.4
  161.4 44.5 reduce-scatter.8
  213.3 34.4 all-gather.6
  249.9 34.4 all-gather.10
  287.9 68.0 reduce-scatter.6
  359.5 66.9 reduce-scatter.10
where the time goes:
time: 436 us
  waiting for transfers between devices  340 us (78%)
  matrix products  55.4 us (13%)
  between operations  14.2 us (3%)
  local copies, waits for them, and re-layouts  11.7 us (3%)
  other arithmetic  10.7 us (2%)
    reduce_scatter x2, waiting for transfers between devices, unit_sum(): lax.psum_scatter(unit_term().astype(jnp.bfloat16), 'row', scatter_dimensi...  98.6 us
    all_gather x2, waiting for transfers between devices, token_panel(): return lax.all_gather(local_rows, 'row', axis=0, tiled=True)  94 us
    reduce_scatter x2, waiting for transfers between devices, width_split(): lax.psum_scatter(width_term().astype(jnp.bfloat16), 'col', scatter_dimens...  84.4 us
    all_gather x2, waiting for transfers between devices, hidden_panel(): return lax.all_gather(local_rows, 'col', axis=0, tiled=True)  61 us
    dot_general x2, matrix products, contract_last(): lax.dot_general(left, right, (((1,), (1,)), ((), ())), preferred_element_...  18.7 us
    unnamed x9, local copies, waits for them, and re-layouts  11 us
    dot_general x1, matrix products, width_term(): return jnp.dot(left_all, right, preferred_element_type=jnp.float32)  9.33 us
    dot_general x1, matrix products, unit_term(): return jnp.dot(left_all, right, preferred_element_type=jnp.float32)  9.31 us
  transfers between devices with their start and end apart: 9, of which 8 were waited for; matrix products, arithmetic and copies ran while one was open for 16% of the time, Pallas kernels for 0%

commit v1 on v0

v1 whole, which is shorter than its diff:
```python
import jax
import jax.numpy as jnp
from jax import lax
from jax.sharding import PartitionSpec as P

CORES = 2
F32 = jnp.float32
BF16 = jnp.bfloat16


def ring_order(count):
    if count % 4:
        return list(range(count))
    minor = count // 4
    order = [major * minor for major in range(4)]
    for turn, major in enumerate(reversed(range(4))):
        steps = range(1, minor) if turn % 2 == 0 else range(minor - 1, 0, -1)
        order += [major * minor + step for step in steps]
    return order


def ring_pairs(count, n_col, sign):
    order = ring_order(count)
    pairs = []
    for place in range(count):
        for col in range(n_col):
            step = sign if col % CORES == 0 else -sign
            target = order[(place + step) % count]
            pairs.append((order[place] * n_col + col, target * n_col + col))
    return pairs


def gelu_parts(value):
    cdf = 0.5 * (1.0 + lax.erf(value * 0.7071067811865476))
    pdf = jnp.exp(-0.5 * value * value) * 0.3989422804014327
    return (value * cdf).astype(BF16), (cdf + value * pdf).astype(BF16)


def dot_nn(left, right):
    return jnp.dot(left, right, preferred_element_type=F32)


def dot_nt(left, right):
    return lax.dot_general(left, right, (((1,), (1,)), ((), ())), preferred_element_type=F32)


def dot_tn(left, right):
    return lax.dot_general(left, right, (((0,), (0,)), ((), ())), preferred_element_type=F32)


def solution(mesh):
    n_row, n_col = mesh.shape["row"], mesh.shape["col"]
    n_x = n_col // CORES
    far = n_row // 2
    ring_a = ring_pairs(n_row, n_col, 1)
    ring_b = ring_pairs(n_row, n_col, -1)
    sibling = [(col, col ^ 1) for col in range(n_col)]
    chip_ring = [(col, (col + CORES) % n_col) for col in range(n_col)]

    def along(value, pairs):
        return lax.ppermute(value, ("row", "col"), pairs)

    def to_sibling(value):
        return lax.ppermute(value, "col", sibling)

    def local(tokens, w_in, w_out, cotangent):
        half = tokens.shape[0] // 2
        core = lax.axis_index("col") % CORES

        def shares(block):
            low, high = block[:half], block[half:]
            return jnp.where(core == 0, low, high), jnp.where(core == 0, high, low)

        def joined(mine, other):
            return jnp.concatenate([jnp.where(core == 0, mine, other), jnp.where(core == 0, other, mine)])

        def gather(block):
            mine, other = shares(block)
            a, b = [mine], [other]
            cur_a = cur_b = block
            for step in range(1, far + 1):
                if step == far:
                    cur_a, cur_b = shares(cur_a)[0], shares(cur_b)[1]
                cur_a, cur_b = along(cur_a, ring_a), along(cur_b, ring_b)
                a.append(cur_a)
                b.append(cur_b)
            return a, b

        def width_sum(mine, other, product):
            got = to_sibling(product(other).astype(BF16))
            chip = (product(mine) + got.astype(F32)).astype(BF16)
            total = chip.astype(F32)
            for _ in range(n_x - 1):
                chip = lax.ppermute(chip, "col", chip_ring)
                total = total + chip.astype(F32)
            return total

        def unit_sum(share_a, share_b, product, own):
            go_a = along(product(share_b[far]).astype(BF16), ring_a)
            go_b = along(product(share_a[far]).astype(BF16), ring_b)
            for step in range(far - 1, 0, -1):
                part_a, part_b = product(share_b[step]), product(share_a[step])
                if step == far - 1:
                    pad = jnp.zeros_like(go_a)
                    go_a, go_b = joined(pad, go_a), joined(go_b, pad)
                go_a = along((part_a + go_a.astype(F32)).astype(BF16), ring_a)
                go_b = along((part_b + go_b.astype(F32)).astype(BF16), ring_b)
            rest = product(joined(share_a[0], share_b[0]))
            total = own.astype(F32) + rest + go_a.astype(F32) + go_b.astype(F32)
            return total.astype(BF16)

        tok_a, tok_b = gather(tokens)
        cot_a, cot_b = gather(cotangent)

        act_a, act_b, slope_a = {}, {}, {}
        for step in range(far + 1):
            pre = width_sum(tok_a[step], tok_b[step], lambda rows: dot_nn(rows, w_in))
            act_a[step], slope_a[step] = gelu_parts(pre)
            act_b[step] = to_sibling(act_a[step])

        mixed = unit_sum(act_a, act_b, lambda rows: dot_nn(rows, w_out), tokens)
        block_out = lax.all_to_all(mixed, "col", split_axis=0, concat_axis=1, tiled=True)

        dpre_a, dpre_b = {}, {}
        for step in range(far, -1, -1):
            dact = width_sum(cot_a[step], cot_b[step], lambda rows: dot_nt(rows, w_out))
            dpre_a[step] = (dact * slope_a[step].astype(F32)).astype(BF16)
            dpre_b[step] = to_sibling(dpre_a[step])

        back = unit_sum(dpre_a, dpre_b, lambda rows: dot_nt(rows, w_in), cotangent)

        def whole(a, b):
            return jnp.concatenate([p for step in range(far + 1) for p in (a[step], b[step])])

        grad_out = dot_tn(whole(act_a, act_b), whole(cot_a, cot_b))
        grad_in = dot_tn(whole(tok_a, tok_b), whole(dpre_a, dpre_b))
        return block_out, back, grad_in, grad_out

    in_specs = (P("row", "col"), P("col", "row"), P("row", "col"), P("row", "col"))
    out_specs = (P(("row", "col"), None), P("row", "col"), P("col", "row"), P("row", "col"))
    return jax.shard_map(local, mesh=mesh, in_specs=in_specs, out_specs=out_specs, check_vma=False)
```

time: 436 us -> 235 us (0.54)
  waiting for transfers between devices: 340 us -> 92.7 us
  starting transfers between devices: 3.91 us -> 70 us
  between operations: 14.2 us -> 1.66 us
  local copies, waits for them, and re-layouts: 11.7 us -> 1.35 us
  other arithmetic: 10.7 us -> 3.27 us
  matrix products: 55.4 us -> 62.3 us
    reduce_scatter x4 -> x0, waiting for transfers between devices: 183 us -> none  [the longest x2 98.6 us: unit_sum(): lax.psum_scatter(unit_term().astype(jnp.bfloat16), 'row', scatter_dimensi...]
    all_gather x4 -> x0, waiting for transfers between devices: 155 us -> none  [the longest x2 94 us: token_panel(): return lax.all_gather(local_rows, 'row', axis=0, tiled=True)]
    ppermute x0 -> x62, waiting for transfers between devices: none -> 91.2 us  [the longest x10 56.6 us: width_sum(): chip = lax.ppermute(chip, 'col', chip_ring)]
    ppermute x0 -> x62, starting transfers between devices: none -> 66.5 us  [the longest x32 50.1 us: along(): return lax.ppermute(value, ('row', 'col'), pairs)]
    convert_element_type x3 -> x0, other arithmetic: 10.7 us -> none  [the longest x1 7.29 us: local(): (dact_part * gelu_grad(pre_part)).astype(jnp.bfloat16)]
    unnamed x9 -> x28, local copies, waits for them, and re-layouts: 11 us -> 0.58 us
    dot_general x6 -> x40, matrix products: 55.4 us -> 62.3 us  [the longest x19 31 us: dot_nt(): lax.dot_general(left, right, (((1,), (1,)), ((), ())), preferred_element_...]
  transfers between devices with their start and end apart: 9 -> 63, of which waited for: 8 -> 25; matrix products, arithmetic and copies ran while one was open for 16% -> 28% of each run, Pallas kernels for 0% -> 0%
where the time goes in v1:
time: 235 us; the launch traced here: 231 us
  waiting for transfers between devices  92.7 us (39%)
  starting transfers between devices  70 us (30%)
  matrix products  62.3 us (27%)
  other arithmetic  3.27 us (1%)
    ppermute x10, waiting for transfers between devices, width_sum(): chip = lax.ppermute(chip, 'col', chip_ring)  56.6 us
    ppermute x32, starting transfers between devices, along(): return lax.ppermute(value, ('row', 'col'), pairs)  50.1 us
    ppermute x32, waiting for transfers between devices, along(): return lax.ppermute(value, ('row', 'col'), pairs)  34.2 us
    dot_general x19, matrix products, dot_nt(): lax.dot_general(left, right, (((1,), (1,)), ((), ())), preferred_element_...  31 us
    dot_general x19, matrix products, dot_nn(): return jnp.dot(left, right, preferred_element_type=F32)  17.7 us
    dot_general x2, matrix products, dot_tn(): lax.dot_general(left, right, (((0,), (0,)), ((), ())), preferred_element_...  13.6 us
    ppermute x10, starting transfers between devices, width_sum(): chip = lax.ppermute(chip, 'col', chip_ring)  12.2 us
  transfers between devices with their start and end apart: 63, of which 25 were waited for; matrix products, arithmetic and copies ran while one was open for 28% of the time, Pallas kernels for 0%

profile of v1, /device:TPU:0, one launch (start us, length us, event | category | flops | bytes accessed | tf_op | source)
XLA Modules:
  0.0 231.3 jit_solution(8982885534255086252)
XLA Ops:
  0.7 3.1 %collective-permute-start.3 = (bf16[128,1024]{1,0:T(8,128)(2,1)}, bf16[128,1024]{1,0:T(8,128)(2,1)S(1)}, u32[]{:S(2)}, u32[]{:S(2)}) collective-permute-start(bf16[128,1024]{1,0:T(8,128)(2,1)} %param.4), channel_id=1, source_target_pairs={{0,8},{1,5},{2,10},{3,7},{8,16},{9,1},{10,18},{11,3},{16,24},{17,9... | collective-permute-start | bytes 786440 | tf_op jit(solution)/shard_map/ppermute | solution.py:61
  3.7 2.0 collective-permute-start.34
  5.8 3.3 %convolution_convert_fusion.9 = bf16[64,2048]{1,0:T(8,128)(2,1)S(1)} fusion(bf16[1024,2048]{1,0:T(8,128)(2,1)} %param.5, pred[]{:T(512)S(6)} %eq.4, bf16[128,1024]{1,0:T(8,128)(2,1)} %param.4), kind=kOutput, calls=%fused_computation.25 | convolution fusion | flops 268632064 | bytes 4718593 | tf_op jit(solution)/shard_map/dot_general | solution.py:40
  18.9 2.1 collective-permute-start.8
  23.6 3.3 %collective-permute-done.32 = bf16[64,2048]{1,0:T(8,128)(2,1)S(1)} collective-permute-done((bf16[64,2048]{1,0:T(8,128)(2,1)S(1)}, bf16[64,2048]{1,0:T(8,128)(2,1)S(1)}, u32[]{:S(2)}, u32[]{:S(2)}) %collective-permute-start.32) | collective-permute-done | bytes 262176 | tf_op jit(solution)/shard_map/ppermute | solution.py:94
  30.4 5.1 %collective-permute-done.40 = bf16[128,1024]{1,0:T(8,128)(2,1)S(1)} collective-permute-done((bf16[128,1024]{1,0:T(8,128)(2,1)S(1)}, bf16[128,1024]{1,0:T(8,128)(2,1)S(1)}, u32[]{:S(2)}, u32[]{:S(2)}) %collective-permute-start.40) | collective-permute-done | bytes 262176 | tf_op jit(solution)/shard_map/ppermute | solution.py:61
  42.2 3.1 %collective-permute-done.14 = bf16[128,1024]{1,0:T(8,128)(2,1)S(1)} collective-permute-done((bf16[128,1024]{1,0:T(8,128)(2,1)S(1)}, bf16[128,1024]{1,0:T(8,128)(2,1)S(1)}, u32[]{:S(2)}, u32[]{:S(2)}) %collective-permute-start.14) | collective-permute-done | bytes 262176 | tf_op jit(solution)/shard_map/ppermute | solution.py:61
  47.8 3.9 %collective-permute-done.45 = bf16[128,1024]{1,0:T(8,128)(2,1)S(1)} collective-permute-done((bf16[128,1024]{1,0:T(8,128)(2,1)S(1)}, bf16[128,1024]{1,0:T(8,128)(2,1)S(1)}, u32[]{:S(2)}, u32[]{:S(2)}) %collective-permute-start.45) | collective-permute-done | bytes 262176 | tf_op jit(solution)/shard_map/ppermute | solution.py:61
  64.6 4.4 %collective-permute-done.19 = bf16[64,1024]{1,0:T(8,128)(2,1)S(1)} collective-permute-done((bf16[64,1024]{1,0:T(8,128)(2,1)S(1)}, bf16[64,1024]{1,0:T(8,128)(2,1)S(1)}, u32[]{:S(2)}, u32[]{:S(2)}) %collective-permute-start.19) | collective-permute-done | bytes 131104 | tf_op jit(solution)/shard_map/ppermute | solution.py:61
  71.1 3.7 %collective-permute-done.18 = bf16[64,1024]{1,0:T(8,128)(2,1)S(1)} collective-permute-done((bf16[64,1024]{1,0:T(8,128)(2,1)S(1)}, bf16[64,1024]{1,0:T(8,128)(2,1)S(1)}, u32[]{:S(2)}, u32[]{:S(2)}) %collective-permute-start.18) | collective-permute-done | bytes 131104 | tf_op jit(solution)/shard_map/ppermute | solution.py:61
  76.3 3.5 %collective-permute-done.50 = bf16[64,1024]{1,0:T(8,128)(2,1)S(1)} collective-permute-done((bf16[64,1024]{1,0:T(8,128)(2,1)S(1)}, bf16[64,1024]{1,0:T(8,128)(2,1)S(1)}, u32[]{:S(2)}, u32[]{:S(2)}) %collective-permute-start.50) | collective-permute-done | bytes 131104 | tf_op jit(solution)/shard_map/ppermute | solution.py:61
  88.9 10.4 %collective-permute-done.11 = bf16[128,2048]{1,0:T(8,128)(2,1)S(1)} collective-permute-done((bf16[128,2048]{1,0:T(8,128)(2,1)S(1)}, bf16[128,2048]{1,0:T(8,128)(2,1)S(1)}, u32[]{:S(2)}, u32[]{:S(2)}) %collective-permute-start.11) | collective-permute-done | bytes 524320 | tf_op jit(solution)/shard_map/ppermute | solution.py:94
  99.3 10.4 %collective-permute-done.42 = bf16[128,2048]{1,0:T(8,128)(2,1)S(1)} collective-permute-done((bf16[128,2048]{1,0:T(8,128)(2,1)S(1)}, bf16[128,2048]{1,0:T(8,128)(2,1)S(1)}, u32[]{:S(2)}, u32[]{:S(2)}) %collective-permute-start.42) | collective-permute-done | bytes 524320 | tf_op jit(solution)/shard_map/ppermute | solution.py:94
  115.3 10.7 %collective-permute-done.16 = bf16[128,2048]{1,0:T(8,128)(2,1)S(1)} collective-permute-done((bf16[128,2048]{1,0:T(8,128)(2,1)S(1)}, bf16[128,2048]{1,0:T(8,128)(2,1)S(1)}, u32[]{:S(2)}, u32[]{:S(2)}) %collective-permute-start.16) | collective-permute-done | bytes 524320 | tf_op jit(solution)/shard_map/ppermute | solution.py:94
  126.0 10.8 %collective-permute-done.47 = bf16[128,2048]{1,0:T(8,128)(2,1)S(1)} collective-permute-done((bf16[128,2048]{1,0:T(8,128)(2,1)S(1)}, bf16[128,2048]{1,0:T(8,128)(2,1)S(1)}, u32[]{:S(2)}, u32[]{:S(2)}) %collective-permute-start.47) | collective-permute-done | bytes 524320 | tf_op jit(solution)/shard_map/ppermute | solution.py:94
  142.4 5.3 %collective-permute-done.21 = bf16[64,2048]{1,0:T(8,128)(2,1)S(1)} collective-permute-done((bf16[64,2048]{1,0:T(8,128)(2,1)S(1)}, bf16[64,2048]{1,0:T(8,128)(2,1)S(1)}, u32[]{:S(2)}, u32[]{:S(2)}) %collective-permute-start.21) | collective-permute-done | bytes 262176 | tf_op jit(solution)/shard_map/ppermute | solution.py:94
  147.6 5.2 %collective-permute-done.52 = bf16[64,2048]{1,0:T(8,128)(2,1)S(1)} collective-permute-done((bf16[64,2048]{1,0:T(8,128)(2,1)S(1)}, bf16[64,2048]{1,0:T(8,128)(2,1)S(1)}, u32[]{:S(2)}, u32[]{:S(2)}) %collective-permute-start.52) | collective-permute-done | bytes 262176 | tf_op jit(solution)/shard_map/ppermute | solution.py:94
  159.6 9.3 %collective-permute-start.23 = (bf16[64,1024]{1,0:T(8,128)(2,1)S(1)}, bf16[64,1024]{1,0:T(8,128)(2,1)S(1)}, u32[]{:S(2)}, u32[]{:S(2)}) collective-permute-start(bf16[64,1024]{1,0:T(8,128)(2,1)S(1)} %convolution_convert_fusion.13), channel_id=1, source_target_pairs={{0,8},{1,5},{2,10},{3,7},{8,16},{9,1},{10,18},{11,3},{16,24},{17,9... | collective-permute-start | bytes 393224 | tf_op jit(solution)/shard_map/ppermute | solution.py:61
  171.6 6.8 %fusion.61 = f32[1024,2048]{1,0:T(8,128)} fusion(bf16[1024,1024]{1,0:T(8,128)(2,1)S(1)} %constant_dynamic-update-slice_fusion, bf16[1024,2048]{1,0:T(8,128)(2,1)S(1)} %constant_dynamic-update-slice_fusion.10), kind=kOutput, calls=%fused_computation.184 | convolution fusion | flops 4294967296 | bytes 14680064 | tf_op jit(solution)/shard_map/dot_general | solution.py:48
  178.4 6.8 %fusion.62 = f32[2048,1024]{1,0:T(8,128)} fusion(bf16[1024,2048]{1,0:T(8,128)(2,1)S(1)} %constant_dynamic-update-slice_fusion.20, bf16[1024,1024]{1,0:T(8,128)(2,1)S(1)} %constant_dynamic-update-slice_fusion.30), kind=kOutput, calls=%fused_computation.185 | convolution fusion | flops 4294967296 | bytes 14680064 | tf_op jit(solution)/shard_map/dot_general | solution.py:48
  198.9 2.0 collective-permute-done.59
  210.1 2.0 collective-permute-done.60
  220.9 3.4 %all-to-all-start = ((bf16[4,32,1024]{2,1,0:T(8,128)(2,1)}), bf16[4,32,1024]{2,1,0:T(8,128)(2,1)S(1)}, u32[]{:S(2)}, u32[]{:S(2)}) async-start(bf16[4,32,1024]{2,1,0:T(8,128)(2,1)} %bitcast), calls=%async_computation | async-start | bytes 524288 | tf_op jit(solution)/shard_map/all_to_all | solution.py:122
  224.3 4.5 %fusion.12 = bf16[128,1024]{1,0:T(8,128)(2,1)} fusion(bf16[1024,2048]{1,0:T(8,128)(2,1)} %param.5, bf16[64,2048]{1,0:T(8,128)(2,1)S(1)} %get-tuple-element.33, bf16[64,2048]{1,0:T(8,128)(2,1)S(1)} %get-tuple-element.32, bf16[128,1024]{1,0:T(8,128)(2,1)S(1)} %collective-permute-done.61, bf16[128,1024]{1,0:T(8,128)(2,1)S(1)} %collective-permute-done.57, ...), kind=kOutput, calls=%fused_computation.47 | convolution fusion | flops 538836992 | bytes 5767168 | tf_op jit(solution)/shard_map/dot_general | solution.py:44
  (192 shorter events, 104.5 us)
Async XLA Ops:
  0.7 17.7 %collective-permute-start.3 = (bf16[128,1024]{1,0:T(8,128)(2,1)}, bf16[128,1024]{1,0:T(8,128)(2,1)S(1)}, u32[]{:S(2)}, u32[]{:S(2)}) collective-permute-start(bf16[128,1024]{1,0:T(8,128)(2,1)} %param.4), channel_id=1, source_target_pairs={{0,8},{1,5},{2,10},{3,7},{8,16},{9,1},{10,18},{11,3},{16,24},{17,9... | collective-permute-start | bytes 786440 | tf_op jit(solution)/shard_map/ppermute | solution.py:61
  3.7 15.2 %collective-permute-start.34 = (bf16[128,1024]{1,0:T(8,128)(2,1)}, bf16[128,1024]{1,0:T(8,128)(2,1)S(1)}, u32[]{:S(2)}, u32[]{:S(2)}) collective-permute-start(bf16[128,1024]{1,0:T(8,128)(2,1)} %param.7), channel_id=1, source_target_pairs={{0,8},{1,5},{2,10},{3,7},{8,16},{9,1},{10,18},{11,3},{16,24},{17,9... | collective-permute-start | bytes 786440 | tf_op jit(solution)/shard_map/ppermute | solution.py:61
  16.7 20.9 %collective-permute-start.5 = (bf16[128,2048]{1,0:T(8,128)(2,1)S(1)}, bf16[128,2048]{1,0:T(8,128)(2,1)S(1)}, u32[]{:S(2)}, u32[]{:S(2)}) collective-permute-start(bf16[128,2048]{1,0:T(8,128)(2,1)S(1)} %convolution_convert_fusion.5), channel_id=1, source_target_pairs={{0,1},{1,0},{2,3},{3,2},{4,5},{5,4},{6,7},{7,6},{8,9},{9,8},{10,11... | collective-permute-start | bytes 1572872 | tf_op jit(solution)/shard_map/ppermute | solution.py:64
  18.3 20.5 %collective-permute-start.36 = (bf16[128,2048]{1,0:T(8,128)(2,1)S(1)}, bf16[128,2048]{1,0:T(8,128)(2,1)S(1)}, u32[]{:S(2)}, u32[]{:S(2)}) collective-permute-start(bf16[128,2048]{1,0:T(8,128)(2,1)S(1)} %convolution_convert_fusion.2), channel_id=1, source_target_pairs={{0,1},{1,0},{2,3},{3,2},{4,5},{5,4},{6,7},{7,6},{8,9},{9,8},{10,11... | collective-permute-start | bytes 1572872 | tf_op jit(solution)/shard_map/ppermute | solution.py:64
  29.6 25.1 %collective-permute-start.2 = (bf16[64,2048]{1,0:T(8,128)(2,1)S(1)}, bf16[64,2048]{1,0:T(8,128)(2,1)S(1)}, u32[]{:S(2)}, u32[]{:S(2)}) collective-permute-start(bf16[64,2048]{1,0:T(8,128)(2,1)S(1)} %get-tuple-element.35), channel_id=1, source_target_pairs={{0,1},{1,0},{2,3},{3,2},{4,5},{5,4},{6,7},{7,6},{8,9},{9,8},{10,11... | collective-permute-start | bytes 786440 | tf_op jit(solution)/shard_map/ppermute | solution.py:64
  35.5 27.4 %collective-permute-start.33 = (bf16[64,2048]{1,0:T(8,128)(2,1)S(1)}, bf16[64,2048]{1,0:T(8,128)(2,1)S(1)}, u32[]{:S(2)}, u32[]{:S(2)}) collective-permute-start(bf16[64,2048]{1,0:T(8,128)(2,1)S(1)} %get-tuple-element.23), channel_id=1, source_target_pairs={{0,1},{1,0},{2,3},{3,2},{4,5},{5,4},{6,7},{7,6},{8,9},{9,8},{10,11... | collective-permute-start | bytes 786440 | tf_op jit(solution)/shard_map/ppermute | solution.py:64
  37.4 46.3 %collective-permute-start.10 = (bf16[128,2048]{1,0:T(8,128)(2,1)S(1)}, bf16[128,2048]{1,0:T(8,128)(2,1)S(1)}, u32[]{:S(2)}, u32[]{:S(2)}) collective-permute-start(bf16[128,2048]{1,0:T(8,128)(2,1)S(1)} %convolution_convert_fusion.4), channel_id=1, source_target_pairs={{0,1},{1,0},{2,3},{3,2},{4,5},{5,4},{6,7},{7,6},{8,9},{9,8},{10,11... | collective-permute-start | bytes 1572872 | tf_op jit(solution)/shard_map/ppermute | solution.py:64
  37.7 47.4 %collective-permute-start.41 = (bf16[128,2048]{1,0:T(8,128)(2,1)S(1)}, bf16[128,2048]{1,0:T(8,128)(2,1)S(1)}, u32[]{:S(2)}, u32[]{:S(2)}) collective-permute-start(bf16[128,2048]{1,0:T(8,128)(2,1)S(1)} %convolution_convert_fusion.1), channel_id=1, source_target_pairs={{0,1},{1,0},{2,3},{3,2},{4,5},{5,4},{6,7},{7,6},{8,9},{9,8},{10,11... | collective-permute-start | bytes 1572872 | tf_op jit(solution)/shard_map/ppermute | solution.py:64
  58.3 23.0 %collective-permute-start.6 = (bf16[128,2048]{1,0:T(8,128)(2,1)S(1)}, bf16[128,2048]{1,0:T(8,128)(2,1)S(1)}, u32[]{:S(2)}, u32[]{:S(2)}) collective-permute-start(bf16[128,2048]{1,0:T(8,128)(2,1)S(1)} %fusion), channel_id=1, source_target_pairs={{0,2},{1,3},{2,0},{3,1},{4,6},{5,7},{6,4},{7,5},{8,10},{9,11},{10,... | collective-permute-start | bytes 1572872 | tf_op jit(solution)/shard_map/ppermute | solution.py:94
  61.1 21.5 %collective-permute-start.37 = (bf16[128,2048]{1,0:T(8,128)(2,1)S(1)}, bf16[128,2048]{1,0:T(8,128)(2,1)S(1)}, u32[]{:S(2)}, u32[]{:S(2)}) collective-permute-start(bf16[128,2048]{1,0:T(8,128)(2,1)S(1)} %fusion.3), channel_id=1, source_target_pairs={{0,2},{1,3},{2,0},{3,1},{4,6},{5,7},{6,4},{7,5},{8,10},{9,11},{10,... | collective-permute-start | bytes 1572872 | tf_op jit(solution)/shard_map/ppermute | solution.py:94
  79.8 30.7 %collective-permute-start.15 = (bf16[128,2048]{1,0:T(8,128)(2,1)S(1)}, bf16[128,2048]{1,0:T(8,128)(2,1)S(1)}, u32[]{:S(2)}, u32[]{:S(2)}) collective-permute-start(bf16[128,2048]{1,0:T(8,128)(2,1)S(1)} %convolution_convert_fusion.3), channel_id=1, source_target_pairs={{0,1},{1,0},{2,3},{3,2},{4,5},{5,4},{6,7},{7,6},{8,9},{9,8},{10,11... | collective-permute-start | bytes 1572872 | tf_op jit(solution)/shard_map/ppermute | solution.py:64
  84.5 14.8 %collective-permute-start.11 = (bf16[128,2048]{1,0:T(8,128)(2,1)S(1)}, bf16[128,2048]{1,0:T(8,128)(2,1)S(1)}, u32[]{:S(2)}, u32[]{:S(2)}) collective-permute-start(bf16[128,2048]{1,0:T(8,128)(2,1)S(1)} %fusion.1), channel_id=1, source_target_pairs={{0,2},{1,3},{2,0},{3,1},{4,6},{5,7},{6,4},{7,5},{8,10},{9,11},{10,... | collective-permute-start | bytes 1572872 | tf_op jit(solution)/shard_map/ppermute | solution.py:94
  86.6 23.1 %collective-permute-start.42 = (bf16[128,2048]{1,0:T(8,128)(2,1)S(1)}, bf16[128,2048]{1,0:T(8,128)(2,1)S(1)}, u32[]{:S(2)}, u32[]{:S(2)}) collective-permute-start(bf16[128,2048]{1,0:T(8,128)(2,1)S(1)} %fusion.4), channel_id=1, source_target_pairs={{0,2},{1,3},{2,0},{3,1},{4,6},{5,7},{6,4},{7,5},{8,10},{9,11},{10,... | collective-permute-start | bytes 1572872 | tf_op jit(solution)/shard_map/ppermute | solution.py:94
  88.2 23.8 %collective-permute-start.46 = (bf16[128,2048]{1,0:T(8,128)(2,1)S(1)}, bf16[128,2048]{1,0:T(8,128)(2,1)S(1)}, u32[]{:S(2)}, u32[]{:S(2)}) collective-permute-start(bf16[128,2048]{1,0:T(8,128)(2,1)S(1)} %convolution_convert_fusion), channel_id=1, source_target_pairs={{0,1},{1,0},{2,3},{3,2},{4,5},{5,4},{6,7},{7,6},{8,9},{9,8},{10,11... | collective-permute-start | bytes 1572872 | tf_op jit(solution)/shard_map/ppermute | solution.py:64
  88.5 49.1 %collective-permute-start.20 = (bf16[64,2048]{1,0:T(8,128)(2,1)S(1)}, bf16[64,2048]{1,0:T(8,128)(2,1)S(1)}, u32[]{:S(2)}, u32[]{:S(2)}) collective-permute-start(bf16[64,2048]{1,0:T(8,128)(2,1)S(1)} %convolution_convert_fusion.8), channel_id=1, source_target_pairs={{0,1},{1,0},{2,3},{3,2},{4,5},{5,4},{6,7},{7,6},{8,9},{9,8},{10,11... | collective-permute-start | bytes 786440 | tf_op jit(solution)/shard_map/ppermute | solution.py:64
  111.2 14.8 %collective-permute-start.16 = (bf16[128,2048]{1,0:T(8,128)(2,1)S(1)}, bf16[128,2048]{1,0:T(8,128)(2,1)S(1)}, u32[]{:S(2)}, u32[]{:S(2)}) collective-permute-start(bf16[128,2048]{1,0:T(8,128)(2,1)S(1)} %fusion.2), channel_id=1, source_target_pairs={{0,2},{1,3},{2,0},{3,1},{4,6},{5,7},{6,4},{7,5},{8,10},{9,11},{10,... | collective-permute-start | bytes 1572872 | tf_op jit(solution)/shard_map/ppermute | solution.py:94
  113.5 23.3 %collective-permute-start.47 = (bf16[128,2048]{1,0:T(8,128)(2,1)S(1)}, bf16[128,2048]{1,0:T(8,128)(2,1)S(1)}, u32[]{:S(2)}, u32[]{:S(2)}) collective-permute-start(bf16[128,2048]{1,0:T(8,128)(2,1)S(1)} %fusion.5), channel_id=1, source_target_pairs={{0,2},{1,3},{2,0},{3,1},{4,6},{5,7},{6,4},{7,5},{8,10},{9,11},{10,... | collective-permute-start | bytes 1572872 | tf_op jit(solution)/shard_map/ppermute | solution.py:94
  115.1 24.2 %collective-permute-start.51 = (bf16[64,2048]{1,0:T(8,128)(2,1)S(1)}, bf16[64,2048]{1,0:T(8,128)(2,1)S(1)}, u32[]{:S(2)}, u32[]{:S(2)}) collective-permute-start(bf16[64,2048]{1,0:T(8,128)(2,1)S(1)} %convolution_convert_fusion.6), channel_id=1, source_target_pairs={{0,1},{1,0},{2,3},{3,2},{4,5},{5,4},{6,7},{7,6},{8,9},{9,8},{10,11... | collective-permute-start | bytes 786440 | tf_op jit(solution)/shard_map/ppermute | solution.py:64
  140.7 12.2 %collective-permute-start.52 = (bf16[64,2048]{1,0:T(8,128)(2,1)S(1)}, bf16[64,2048]{1,0:T(8,128)(2,1)S(1)}, u32[]{:S(2)}, u32[]{:S(2)}) collective-permute-start(bf16[64,2048]{1,0:T(8,128)(2,1)S(1)} %fusion.7), channel_id=1, source_target_pairs={{0,2},{1,3},{2,0},{3,1},{4,6},{5,7},{6,4},{7,5},{8,10},{9,11},{10,... | collective-permute-start | bytes 786440 | tf_op jit(solution)/shard_map/ppermute | solution.py:94
  154.2 31.1 %collective-permute-start.27 = (bf16[64,1024]{1,0:T(8,128)(2,1)S(1)}, bf16[64,1024]{1,0:T(8,128)(2,1)S(1)}, u32[]{:S(2)}, u32[]{:S(2)}) collective-permute-start(bf16[64,1024]{1,0:T(8,128)(2,1)S(1)} %convolution_convert_fusion.12), channel_id=1, source_target_pairs={{0,4},{1,9},{2,6},{3,11},{8,0},{9,17},{10,2},{11,19},{16,8},{17,25... | collective-permute-start | bytes 393224 | tf_op jit(solution)/shard_map/ppermute | solution.py:61
  155.7 13.2 %collective-permute-start.53 = (bf16[64,2048]{1,0:T(8,128)(2,1)S(1)}, bf16[64,2048]{1,0:T(8,128)(2,1)S(1)}, u32[]{:S(2)}, u32[]{:S(2)}) collective-permute-start(bf16[64,2048]{1,0:T(8,128)(2,1)S(1)} %get-tuple-element.15), channel_id=1, source_target_pairs={{0,1},{1,0},{2,3},{3,2},{4,5},{5,4},{6,7},{7,6},{8,9},{9,8},{10,11... | collective-permute-start | bytes 786440 | tf_op jit(solution)/shard_map/ppermute | solution.py:64
  157.3 31.6 %collective-permute-start.58 = (bf16[64,1024]{1,0:T(8,128)(2,1)S(1)}, bf16[64,1024]{1,0:T(8,128)(2,1)S(1)}, u32[]{:S(2)}, u32[]{:S(2)}) collective-permute-start(bf16[64,1024]{1,0:T(8,128)(2,1)S(1)} %convolution_convert_fusion.10), channel_id=1, source_target_pairs={{0,4},{1,9},{2,6},{3,11},{8,0},{9,17},{10,2},{11,19},{16,8},{17,25... | collective-permute-start | bytes 393224 | tf_op jit(solution)/shard_map/ppermute | solution.py:61
  159.6 25.6 %collective-permute-start.23 = (bf16[64,1024]{1,0:T(8,128)(2,1)S(1)}, bf16[64,1024]{1,0:T(8,128)(2,1)S(1)}, u32[]{:S(2)}, u32[]{:S(2)}) collective-permute-start(bf16[64,1024]{1,0:T(8,128)(2,1)S(1)} %convolution_convert_fusion.13), channel_id=1, source_target_pairs={{0,8},{1,5},{2,10},{3,7},{8,16},{9,1},{10,18},{11,3},{16,24},{17,9... | collective-permute-start | bytes 393224 | tf_op jit(solution)/shard_map/ppermute | solution.py:61
  170.3 18.6 %collective-permute-start.54 = (bf16[64,1024]{1,0:T(8,128)(2,1)S(1)}, bf16[64,1024]{1,0:T(8,128)(2,1)S(1)}, u32[]{:S(2)}, u32[]{:S(2)}) collective-permute-start(bf16[64,1024]{1,0:T(8,128)(2,1)S(1)} %convolution_convert_fusion.11), channel_id=1, source_target_pairs={{0,8},{1,5},{2,10},{3,7},{8,16},{9,1},{10,18},{11,3},{16,24},{17,9... | collective-permute-start | bytes 393224 | tf_op jit(solution)/shard_map/ppermute | solution.py:61
  (43 other events, 320.2 us)
